TPU v7x, 512 devices: a whole 4x8x8 slice. The times are simulated.
512 devices in a mesh: dp: 8 (over z), seq: 64 (over y, x, core).
Axes of the slice: x: 4, y: 8, z: 8, core: 2. Of those that a mesh axis runs over, the one named last changes fastest.
Arguments:
- tokens: bfloat16 [8, 8192, 1280], P('dp', 'seq'), may hold values from -6 to 6
- place: int32 [64, 128], P('seq'), may hold values from 0 to 127, each once within a row
- kernel: float32 [27, 1280], replicated, may hold values from -1.25 to 1.25
- proj_weight: bfloat16 [1280, 3840], P('seq'), may hold values from -0.15625 to 0.15625
- d_projected: bfloat16 [8, 8192, 3840], P('dp', 'seq'), may hold values from -6 to 6
Outputs:
- projected: bfloat16 [8, 8192, 3840], P('dp', 'seq')
- d_tokens: bfloat16 [8, 8192, 1280], P('dp', 'seq')
- d_kernel: float32 [27, 1280], replicated
Inputs may be any that keep to these rules, and one draw needn't show every extreme that they name: Each row of place holds every number 0 to 127 once.
All inputs are finite; a program needn't handle non-finite values.
Results may differ from a plain program's by a relative error of at most 0.005.
Values may be sent and summed in bfloat16 or wider, within the bound.
No kernel may reach another device: no remote copies, remote signals or barrier semaphores. Data moves between devices by JAX's collectives and lax.ppermute only.
A program may use at most 128 MiB of HBM per device.

v0:
```python
import jax
import jax.numpy as jnp
from jax import lax
from jax.sharding import PartitionSpec as P

INLINE = 8
CROSS = 8


def with_halo(value, sides, width):
    for axis, dim in sides:
        size, length = (lax.axis_size(axis), value.shape[dim])
        up = [(i, (i + 1) % size) for i in range(size - 1)]
        down = [(j, i) for i, j in up]
        last = lax.slice_in_dim(value, length - width, length, axis=dim)
        first = lax.slice_in_dim(value, 0, width, axis=dim)
        before = lax.ppermute(last, axis, up)
        after = lax.ppermute(first, axis, down)
        value = jnp.concatenate([before, value, after], axis=dim)
    return value


def brick_cells(landed, inverse):
    tokens_dev = inverse.shape[0]
    width = landed.shape[-1]
    slots = landed.reshape(tokens_dev, width)
    cells = jnp.take(slots, inverse, axis=0)
    return cells.reshape(tokens_dev // (INLINE * CROSS), INLINE, CROSS, width)


def scan_pieces(cells, order, count):
    width = cells.shape[-1]
    tokens_dev = order.shape[0]
    slots = jnp.take(cells.reshape(tokens_dev, width), order, axis=0)
    return slots.reshape(count, tokens_dev // count, width)


def to_bricks(rows, inverse, count):
    tokens_dev, width = rows.shape
    landed = lax.all_to_all(
        rows.reshape(count, tokens_dev // count, width),
        "seq",
        split_axis=0,
        concat_axis=0,
        tiled=True,
    )
    return brick_cells(landed, inverse)


def to_scan(cells, order, count):
    landed = lax.all_to_all(
        scan_pieces(cells, order, count), "seq", split_axis=0, concat_axis=0, tiled=True
    )
    return landed.reshape(order.shape[0], cells.shape[-1])


def with_faces(block):
    deeper = with_halo(block, (("seq", 0),), 1)
    return jnp.pad(deeper, ((0, 0), (1, 1), (1, 1), (0, 0)))


def window(field, depth_dev, start_z, start_i, start_c):
    return field[
        start_z : start_z + depth_dev, start_i : start_i + INLINE, start_c : start_c + CROSS
    ].astype(jnp.float32)


def forward_conv(grid_x, pad_x, kernel, depth_dev):
    conv = jnp.zeros(grid_x.shape, jnp.float32)
    for offset in range(27):
        conv = conv + kernel[offset] * window(
            pad_x, depth_dev, offset // 9, offset // 3 % 3, offset % 3
        )
    return (grid_x.astype(jnp.float32) + conv).astype(jnp.bfloat16)


def backward_conv(grid_d, pad_d, pad_x, kernel, depth_dev):
    grid_float = grid_d.astype(jnp.float32)
    back = grid_float
    partial_value = []
    for offset in range(27):
        dz, di, dc = (offset // 9, offset // 3 % 3, offset % 3)
        back = back + kernel[offset] * window(pad_d, depth_dev, 2 - dz, 2 - di, 2 - dc)
        partial_value.append(
            jnp.sum(grid_float * window(pad_x, depth_dev, dz, di, dc), axis=(0, 1, 2))
        )
    return (back.astype(jnp.bfloat16), jnp.stack(partial_value))


def shards(tokens, place, kernel, proj_weight, d_projected):
    count = lax.axis_size("seq")
    order = place[0]
    inverse = jnp.argsort(order)
    rows_x = tokens[0]
    d_rows = d_projected[0]
    depth_dev = rows_x.shape[0] // (INLINE * CROSS)
    d_y = lax.dot_general(
        d_rows,
        lax.all_gather(proj_weight, "seq", axis=0, tiled=True),
        (((1,), (1,)), ((), ())),
        preferred_element_type=jnp.float32,
    )
    d_y = d_y.astype(jnp.bfloat16)
    grid_x = to_bricks(rows_x, inverse, count)
    pad_x = with_faces(grid_x)
    grid_y = forward_conv(grid_x, pad_x, kernel, depth_dev)
    rows_y = to_scan(grid_y, order, count)
    grid_d = to_bricks(d_y, inverse, count)
    pad_d = with_faces(grid_d)
    back, partial_value = backward_conv(grid_d, pad_d, pad_x, kernel, depth_dev)
    d_tokens = to_scan(back, order, count)
    projected = jnp.dot(
        rows_y,
        lax.all_gather(proj_weight, "seq", axis=0, tiled=True),
        preferred_element_type=jnp.float32,
    )
    projected = projected.astype(jnp.bfloat16)
    d_kernel = lax.psum(partial_value, ("dp", "seq"))
    return (projected[None], d_tokens[None], d_kernel)


def solution(mesh):
    placed = (P("dp", "seq", None), P("seq", None), P(), P("seq", None), P("dp", "seq", None))
    return jax.shard_map(
        shards,
        mesh=mesh,
        in_specs=placed,
        out_specs=(P("dp", "seq", None), P("dp", "seq", None), P()),
        check_vma=False,
    )
```

profile of v0, /device:TPU:1, one launch (start us, length us, event | category | flops | bytes accessed | tf_op | source)
XLA Modules:
  0.0 491.7 jit_solution(6049392206160936502)
XLA Ops:
  7.2 0.0 copy-start
  7.2 0.0 all-gather.3.cloned.1.call-start
  7.2 0.7 all-gather.3.cloned.1.call-update
  7.9 1.8 reshape_squeeze.3
  9.7 11.6 %all-to-all-start = ((bf16[64,2,1280]{2,1,0:T(2,128)(2,1)}), bf16[64,2,1280]{2,1,0:T(2,128)(2,1)S(1)}, u32[]{:S(2)}, u32[]{:S(2)}) async-start(bf16[64,2,1280]{2,1,0:T(2,128)(2,1)} %reshape_squeeze.3), calls=%async_computation | async-start | bytes 655360 | tf_op jit(solution)/shard_map/all_to_all | solution.py:40
  21.4 3.2 sort.17
  24.6 1.9 slice_reduce_fusion.25
  26.5 0.7 compare_select_fusion
  27.1 83.8 %all-gather.3.cloned.1.call-done = bf16[64,20,3840]{2,1,0:T(8,128)(2,1)} async-done(((bf16[1,20,3840]{2,1,0:T(8,128)(2,1)}), bf16[64,20,3840]{2,1,0:T(8,128)(2,1)}) %all-gather.3.cloned.1.call-update) | async-done | bytes 9830416 | tf_op jit(solution)/shard_map/all_gather | solution.py:114
  110.9 13.7 %reshape.119 = bf16[1280,3840]{1,0:T(8,128)(2,1)} reshape(bf16[64,20,3840]{2,1,0:T(8,128)(2,1)} %all-gather.3.cloned.1.call-done) | data formatting | bytes 19660800
  124.6 0.0 copy-done
  124.6 7.1 %convolution_convert_fusion.1 = bf16[128,1280]{1,0:T(8,128)(2,1)S(1)} fusion(bf16[1280,3840]{1,0:T(8,128)(2,1)} %reshape.119, bf16[1,128,3840]{2,1,0:T(8,128)(2,1)S(1)} %copy-done), kind=kOutput, calls=%fused_computation.41 | convolution fusion | flops 1258455040 | bytes 11141120 | tf_op jit(solution)/shard_map/dot_general | solution.py:97
  131.7 0.9 reshape.77
  132.6 0.0 all-to-all-done
  132.6 5.7 %all-to-all-start.2 = ((bf16[64,2,1280]{2,1,0:T(2,128)(2,1)}), bf16[64,2,1280]{2,1,0:T(2,128)(2,1)S(1)}, u32[]{:S(2)}, u32[]{:S(2)}) async-start(bf16[64,2,1280]{2,1,0:T(2,128)(2,1)} %reshape.77), calls=%async_computation.2 | async-start | bytes 655360 | tf_op jit(solution)/shard_map/all_to_all | solution.py:40
  138.3 0.6 pad_clamp_fusion
  138.8 0.9 slice_reduce_fusion.26
  139.7 0.5 compare_and_fusion
  140.2 0.1 reshape.72
  140.3 0.9 gather_fusion
  141.2 11.2 %all-to-all-done.2 = bf16[64,2,1280]{2,1,0:T(2,128)(2,1)S(1)} async-done(((bf16[64,2,1280]{2,1,0:T(2,128)(2,1)}), bf16[64,2,1280]{2,1,0:T(2,128)(2,1)S(1)}, u32[]{:S(2)}, u32[]{:S(2)}) %all-to-all-start.2) | async-done | bytes 327712 | tf_op jit(solution)/shard_map/all_to_all | solution.py:40
  152.4 0.1 reshape.78
  152.6 0.9 gather_fusion.2
  153.6 0.8 multiply_reduce_fusion
  154.4 2.1 collective-permute-start.1
  156.5 3.5 collective-permute-start
  160.0 0.7 slice_bitcast_fusion.1
  160.7 1.9 collective-permute-start.2
  162.7 3.1 collective-permute-start.3
  165.7 0.0 collective-permute-done.1
  165.7 0.0 collective-permute-done
  165.8 0.6 select_maximum_fusion.2
  166.5 2.5 fusion.83
  168.9 0.0 copy-done.1
  169.0 0.0 copy-done.3
  169.0 1.7 gather_fusion.1
  170.7 0.0 collective-permute-done.2
  170.7 0.0 collective-permute-done.3
  170.7 1.5 select_maximum_fusion
  172.2 3.4 add_convert_fusion
  175.7 1.9 gather_fusion.3
  177.5 1.9 broadcast_select_fusion
  179.5 1.8 reshape.75
  181.3 9.7 %all-to-all-start.1 = ((bf16[64,2,1280]{2,1,0:T(2,128)(2,1)}), bf16[64,2,1280]{2,1,0:T(2,128)(2,1)}, u32[]{:S(2)}, u32[]{:S(2)}) async-start(bf16[64,2,1280]{2,1,0:T(2,128)(2,1)} %reshape.75), calls=%async_computation.1 | async-start | bytes 655360 | tf_op jit(solution)/shard_map/all_to_all | solution.py:51
  190.9 0.0 copy-done.18
  190.9 0.6 stack.97
  191.5 0.8 reshape.81
  192.4 2.4 fusion.82
  194.8 10.2 %all-to-all-done.1 = bf16[64,2,1280]{2,1,0:T(2,128)(2,1)} async-done(((bf16[64,2,1280]{2,1,0:T(2,128)(2,1)}), bf16[64,2,1280]{2,1,0:T(2,128)(2,1)}, u32[]{:S(2)}, u32[]{:S(2)}) %all-to-all-start.1) | async-done | bytes 327712 | tf_op jit(solution)/shard_map/all_to_all | solution.py:51
  205.0 5.2 %all-to-all-start.3 = ((bf16[64,2,1280]{2,1,0:T(2,128)(2,1)}), bf16[64,2,1280]{2,1,0:T(2,128)(2,1)}, u32[]{:S(2)}, u32[]{:S(2)}) async-start(bf16[64,2,1280]{2,1,0:T(2,128)(2,1)} %reshape.81), calls=%async_computation.3 | async-start | bytes 655360 | tf_op jit(solution)/shard_map/all_to_all | solution.py:51
  210.3 0.0 all-reduce.4.cloned.1.call-start
  210.3 1.5 fusion.78
  211.9 0.7 stack.110
  212.7 0.7 stack.109
  213.4 0.7 stack.108
  214.1 0.7 stack.107
  215.0 3.4 stack.111
  218.3 0.0 all-reduce.4.cloned.1.call-update
  218.4 1.1 reshape.76
  219.5 6.2 %fusion = bf16[1,128,3840]{2,1,0:T(8,128)(2,1)} fusion(bf16[128,1280]{1,0:T(8,128)(2,1)S(1)} %reshape.76, bf16[1280,3840]{1,0:T(8,128)(2,1)} %reshape.119), kind=kOutput, calls=%fused_computation.37 | convolution fusion | flops 1258782720 | bytes 11141120 | tf_op jit(solution)/shard_map/dot_general | solution.py:112
  225.7 0.0 all-to-all-done.3
  225.7 1.8 broadcast_in_dim_reshape.3
  227.5 255.8 %all-reduce.4.cloned.1.call-done = f32[27,1280]{1,0:T(8,128)} async-done(((f32[27,1280]{1,0:T(8,128)}), f32[27,1280]{1,0:T(8,128)}) %all-reduce.4.cloned.1.call-update) | async-done | bytes 138256 | tf_op jit(solution)/shard_map/psum | solution.py:118
  483.3 1.6 copy.9
  (62 shorter events, 0.2 us)
Async XLA Ops:
  7.2 117.5 %copy-start = (bf16[1,128,3840]{2,1,0:T(8,128)(2,1)S(1)}, bf16[1,128,3840]{2,1,0:T(8,128)(2,1)}, u32[]{:S(2)}) copy-start(bf16[1,128,3840]{2,1,0:T(8,128)(2,1)} %param.11) | copy-start | bytes 2949124
  7.2 103.8 %all-gather.3.cloned.1.call-start = ((), (), s32[]{:S(2)}) async-start(), calls=%async_computation.5 | async-start | bytes 11980800 | tf_op jit(solution)/shard_map/all_gather | solution.py:114
  9.7 122.8 %all-to-all-start = ((bf16[64,2,1280]{2,1,0:T(2,128)(2,1)}), bf16[64,2,1280]{2,1,0:T(2,128)(2,1)S(1)}, u32[]{:S(2)}, u32[]{:S(2)}) async-start(bf16[64,2,1280]{2,1,0:T(2,128)(2,1)} %reshape_squeeze.3), calls=%async_computation | async-start | bytes 655360 | tf_op jit(solution)/shard_map/all_to_all | solution.py:40
  124.6 14.2 %copy-start.4 = (f32[27,1280]{1,0:T(8,128)S(1)}, f32[27,1280]{1,0:T(8,128)}, u32[]{:S(2)}) copy-start(f32[27,1280]{1,0:T(8,128)} %param.9) | copy-start | bytes 414724
  124.6 15.1 %copy-start.19 = (s32[1,128]{1,0:T(1,128)S(1)}, s32[1,128]{1,0:T(1,128)}, u32[]{:S(2)}) copy-start(s32[1,128]{1,0:T(1,128)} %param.8) | copy-start | bytes 1540
  132.6 19.9 %all-to-all-start.2 = ((bf16[64,2,1280]{2,1,0:T(2,128)(2,1)}), bf16[64,2,1280]{2,1,0:T(2,128)(2,1)S(1)}, u32[]{:S(2)}, u32[]{:S(2)}) async-start(bf16[64,2,1280]{2,1,0:T(2,128)(2,1)} %reshape.77), calls=%async_computation.2 | async-start | bytes 655360 | tf_op jit(solution)/shard_map/all_to_all | solution.py:40
  153.5 12.9 %copy-start.5 = (f32[1280]{0:T(1024)S(1)}, f32[1280]{0:T(1024)}, u32[]{:S(2)}) copy-start(f32[1280]{0:T(1024)} %get-tuple-element.52) | copy-start | bytes 15364
  153.5 12.9 %copy-start.6 = (f32[1280]{0:T(1024)S(1)}, f32[1280]{0:T(1024)}, u32[]{:S(2)}) copy-start(f32[1280]{0:T(1024)} %get-tuple-element.53) | copy-start | bytes 15364
  153.5 12.9 %copy-start.7 = (f32[1280]{0:T(1024)S(1)}, f32[1280]{0:T(1024)}, u32[]{:S(2)}) copy-start(f32[1280]{0:T(1024)} %get-tuple-element.54) | copy-start | bytes 15364
  153.5 12.9 %copy-start.8 = (f32[1280]{0:T(1024)S(1)}, f32[1280]{0:T(1024)}, u32[]{:S(2)}) copy-start(f32[1280]{0:T(1024)} %get-tuple-element.55) | copy-start | bytes 15364
  153.5 12.9 %copy-start.9 = (f32[1280]{0:T(1024)S(1)}, f32[1280]{0:T(1024)}, u32[]{:S(2)}) copy-start(f32[1280]{0:T(1024)} %get-tuple-element.56) | copy-start | bytes 15364
  153.5 12.9 %copy-start.10 = (f32[1280]{0:T(1024)S(1)}, f32[1280]{0:T(1024)}, u32[]{:S(2)}) copy-start(f32[1280]{0:T(1024)} %get-tuple-element.57) | copy-start | bytes 15364
  153.5 12.9 %copy-start.11 = (f32[1280]{0:T(1024)S(1)}, f32[1280]{0:T(1024)}, u32[]{:S(2)}) copy-start(f32[1280]{0:T(1024)} %get-tuple-element.58) | copy-start | bytes 15364
  153.5 12.9 %copy-start.12 = (f32[1280]{0:T(1024)S(1)}, f32[1280]{0:T(1024)}, u32[]{:S(2)}) copy-start(f32[1280]{0:T(1024)} %get-tuple-element.59) | copy-start | bytes 15364
  153.5 12.9 %copy-start.13 = (f32[1280]{0:T(1024)S(1)}, f32[1280]{0:T(1024)}, u32[]{:S(2)}) copy-start(f32[1280]{0:T(1024)} %get-tuple-element.60) | copy-start | bytes 15364
  153.6 12.9 %copy-start.14 = (f32[1280]{0:T(1024)S(1)}, f32[1280]{0:T(1024)}, u32[]{:S(2)}) copy-start(f32[1280]{0:T(1024)} %get-tuple-element.61) | copy-start | bytes 15364
  153.6 12.9 %copy-start.15 = (f32[1280]{0:T(1024)S(1)}, f32[1280]{0:T(1024)}, u32[]{:S(2)}) copy-start(f32[1280]{0:T(1024)} %get-tuple-element.62) | copy-start | bytes 15364
  153.6 12.9 %copy-start.16 = (f32[1280]{0:T(1024)S(1)}, f32[1280]{0:T(1024)}, u32[]{:S(2)}) copy-start(f32[1280]{0:T(1024)} %get-tuple-element.63) | copy-start | bytes 15364
  153.6 12.9 %copy-start.17 = (f32[1280]{0:T(1024)S(1)}, f32[1280]{0:T(1024)}, u32[]{:S(2)}) copy-start(f32[1280]{0:T(1024)} %get-tuple-element.64) | copy-start | bytes 15364
  154.4 14.5 %copy-start.1 = (bf16[128,1280]{1,0:T(8,128)(2,1)}, bf16[128,1280]{1,0:T(8,128)(2,1)S(1)}, u32[]{:S(2)}) copy-start(bf16[128,1280]{1,0:T(8,128)(2,1)S(1)} %get-tuple-element.67) | copy-start | bytes 983044
  154.4 11.3 %collective-permute-start.1 = (bf16[1,8,8,1280]{3,2,1,0:T(8,128)(2,1)S(1)}, bf16[1,8,8,1280]{3,2,1,0:T(8,128)(2,1)S(1)}, u32[]{:S(2)}, u32[]{:S(2)}) collective-permute-start(bf16[1,8,8,1280]{3,2,1,0:T(8,128)(2,1)S(1)} %get-tuple-element.70), channel_id=1, source_target_pairs={{1,0},{2,1},{3,2},{4,3},{5,4},{6,5},{7,6},{8,7},{9,8},{10,9},{11,1... | collective-permute-start | bytes 491528 | tf_op jit(solution)/shard_map/ppermute | solution.py:18
  156.5 9.2 %collective-permute-start = (bf16[1,8,8,1280]{3,2,1,0:T(8,128)(2,1)S(1)}, bf16[1,8,8,1280]{3,2,1,0:T(8,128)(2,1)S(1)}, u32[]{:S(2)}, u32[]{:S(2)}) collective-permute-start(bf16[1,8,8,1280]{3,2,1,0:T(8,128)(2,1)S(1)} %get-tuple-element.71), channel_id=1, source_target_pairs={{0,1},{1,2},{2,3},{3,4},{4,5},{5,6},{6,7},{7,8},{8,9},{9,10},{10,1... | collective-permute-start | bytes 491528 | tf_op jit(solution)/shard_map/ppermute | solution.py:17
  160.7 10.0 %collective-permute-start.2 = (bf16[1,8,8,1280]{3,2,1,0:T(8,128)(2,1)}, bf16[1,8,8,1280]{3,2,1,0:T(8,128)(2,1)}, u32[]{:S(2)}, u32[]{:S(2)}) collective-permute-start(bf16[1,8,8,1280]{3,2,1,0:T(8,128)(2,1)} %get-tuple-element.68), channel_id=1, source_target_pairs={{0,1},{1,2},{2,3},{3,4},{4,5},{5,6},{6,7},{7,8},{8,9},{9,10},{10,1... | collective-permute-start | bytes 491528 | tf_op jit(solution)/shard_map/ppermute | solution.py:17
  162.7 8.0 %collective-permute-start.3 = (bf16[1,8,8,1280]{3,2,1,0:T(8,128)(2,1)}, bf16[1,8,8,1280]{3,2,1,0:T(8,128)(2,1)}, u32[]{:S(2)}, u32[]{:S(2)}) collective-permute-start(bf16[1,8,8,1280]{3,2,1,0:T(8,128)(2,1)} %get-tuple-element.69), channel_id=1, source_target_pairs={{1,0},{2,1},{3,2},{4,3},{5,4},{6,5},{7,6},{8,7},{9,8},{10,9},{11,1... | collective-permute-start | bytes 491528 | tf_op jit(solution)/shard_map/ppermute | solution.py:18
  165.7 3.2 copy-start.3
  175.6 15.3 %copy-start.18 = (f32[1280]{0:T(1024)S(1)}, f32[1280]{0:T(1024)}, u32[]{:S(2)}) copy-start(f32[1280]{0:T(1024)} %get-tuple-element.65) | copy-start | bytes 15364
  181.3 23.8 %all-to-all-start.1 = ((bf16[64,2,1280]{2,1,0:T(2,128)(2,1)}), bf16[64,2,1280]{2,1,0:T(2,128)(2,1)}, u32[]{:S(2)}, u32[]{:S(2)}) async-start(bf16[64,2,1280]{2,1,0:T(2,128)(2,1)} %reshape.75), calls=%async_computation.1 | async-start | bytes 655360 | tf_op jit(solution)/shard_map/all_to_all | solution.py:51
  192.4 18.0 %copy-start.2 = (bf16[128,1280]{1,0:T(8,128)(2,1)S(1)}, bf16[128,1280]{1,0:T(8,128)(2,1)}, u32[]{:S(2)}) copy-start(bf16[128,1280]{1,0:T(8,128)(2,1)} %copy-done.1) | copy-start | bytes 983044
  205.0 20.6 %all-to-all-start.3 = ((bf16[64,2,1280]{2,1,0:T(2,128)(2,1)}), bf16[64,2,1280]{2,1,0:T(2,128)(2,1)}, u32[]{:S(2)}, u32[]{:S(2)}) async-start(bf16[64,2,1280]{2,1,0:T(2,128)(2,1)} %reshape.81), calls=%async_computation.3 | async-start | bytes 655360 | tf_op jit(solution)/shard_map/all_to_all | solution.py:51
  210.3 273.0 %all-reduce.4.cloned.1.call-start = ((), (), s32[]{:S(2)}) async-start(), calls=%async_computation.4 | async-start | bytes 327680 | tf_op jit(solution)/shard_map/psum | solution.py:118
Sparse Core Ops, SparseCore 0:
  11.3 99.6 all-gather.2
  218.5 264.7 all-reduce.3
where the time goes:
time: 493 us; the launch traced here: 492 us
  waiting for transfers between devices  362 us (73%)
  starting transfers between devices  42.8 us (9%)
  local copies, waits for them, and re-layouts  39.6 us (8%)
  other arithmetic  19.6 us (4%)
  between operations  14.6 us (3%)
  matrix products  13.3 us (3%)
    psum x1, waiting for transfers between devices, shards(): d_kernel = lax.psum(partial_value, ('dp', 'seq'))  256 us
    all_gather x1, waiting for transfers between devices, shards(): lax.all_gather(proj_weight, 'seq', axis=0, tiled=True)  83.8 us
    all_to_all x2, starting transfers between devices, to_bricks(): lax.all_to_all(rows.reshape(count, tokens_dev // count, width), 'seq', sp...  17.3 us
    unnamed x42, local copies, waits for them, and re-layouts  15.4 us
    all_to_all x2, starting transfers between devices, to_scan(): lax.all_to_all(scan_pieces(cells, order, count), 'seq', split_axis=0, con...  14.9 us
    all_to_all x2, waiting for transfers between devices, to_bricks(): lax.all_to_all(rows.reshape(count, tokens_dev // count, width), 'seq', sp...  11.2 us
    all_to_all x2, waiting for transfers between devices, to_scan(): lax.all_to_all(scan_pieces(cells, order, count), 'seq', split_axis=0, con...  10.3 us
  transfers between devices with their start and end apart: 10, of which 4 were waited for; matrix products, arithmetic and copies ran while one was open for 12% of the time, Pallas kernels for 0%

commit v1 on v0

--- a/solution.py
+++ b/solution.py
@@ -111,7 +111,9 @@
     d_tokens = to_scan(back, order, count)
     projected = jnp.dot(
         rows_y,
-        lax.all_gather(proj_weight, "seq", axis=0, tiled=True),
+        jnp.concatenate(
+            lax.all_to_all(jnp.stack([proj_weight] * lax.axis_size("seq")), "seq", 0, 0), axis=0
+        ),
         preferred_element_type=jnp.float32,
     )
     projected = projected.astype(jnp.bfloat16)

time: 493 us -> 752 us (1.53)
  waiting for transfers between devices: 362 us -> 577 us
  blocking collectives: 0 us -> 19.7 us
  starting transfers between devices: 42.8 us -> 62.4 us
  local copies, waits for them, and re-layouts: 39.6 us -> 47.5 us
    all_to_all x0 -> x1, waiting for transfers between devices: none -> 199 us  [shards(): lax.all_to_all(jnp.stack([proj_weight] * lax.axis_size('seq')), 'seq', 0, 0)]
    ppermute x2, waiting for transfers between devices: 0.01 us -> 27.1 us  [with_halo(): after = lax.ppermute(first, axis, down)]
    all_to_all x2, starting transfers between devices: 14.9 us -> 35.1 us  [to_scan(): lax.all_to_all(scan_pieces(cells, order, count), 'seq', split_axis=0, con...]
    all_to_all x0 -> x1, blocking collectives: none -> 19.7 us  [to_bricks(): lax.all_to_all(rows.reshape(count, tokens_dev // count, width), 'seq', sp...]
    reshape x0 -> x1, local copies, waits for them, and re-layouts: none -> 13.7 us  [shards(): jnp.concatenate(lax.all_to_all(jnp.stack([proj_weight] * lax.axis_size('s...]
    all_to_all x2 -> x1, waiting for transfers between devices: 11.2 us -> 0.01 us  [to_bricks(): lax.all_to_all(rows.reshape(count, tokens_dev // count, width), 'seq', sp...]
    all_to_all x2 -> x1, starting transfers between devices: 17.3 us -> 11.6 us  [to_bricks(): lax.all_to_all(rows.reshape(count, tokens_dev // count, width), 'seq', sp...]
  transfers between devices with their start and end apart: 10 -> 10, of which waited for: 4 -> 5; matrix products, arithmetic and copies ran while one was open for 12% -> 9% of each run, Pallas kernels for 0% -> 0%
where the time goes in v1:
time: 752 us; the launch traced here: 751 us
  waiting for transfers between devices  577 us (77%)
  starting transfers between devices  62.4 us (8%)
  local copies, waits for them, and re-layouts  47.5 us (6%)
  blocking collectives  19.7 us (3%)
  other arithmetic  16.7 us (2%)
  between operations  14.7 us (2%)
  matrix products  13.4 us (2%)
    psum x1, waiting for transfers between devices, shards(): d_kernel = lax.psum(partial_value, ('dp', 'seq'))  256 us
    all_to_all x1, waiting for transfers between devices, shards(): lax.all_to_all(jnp.stack([proj_weight] * lax.axis_size('seq')), 'seq', 0, 0)  199 us
    all_gather x1, waiting for transfers between devices, shards(): lax.all_gather(proj_weight, 'seq', axis=0, tiled=True)  89.6 us
    all_to_all x2, starting transfers between devices, to_scan(): lax.all_to_all(scan_pieces(cells, order, count), 'seq', split_axis=0, con...  35.1 us
    ppermute x2, waiting for transfers between devices, with_halo(): after = lax.ppermute(first, axis, down)  27.1 us
    all_to_all x1, blocking collectives, to_bricks(): lax.all_to_all(rows.reshape(count, tokens_dev // count, width), 'seq', sp...  19.7 us
    unnamed x42, local copies, waits for them, and re-layouts  15.4 us
  transfers between devices with their start and end apart: 10, of which 5 were waited for; matrix products, arithmetic and copies ran while one was open for 9% of the time, Pallas kernels for 0%

profile of v1, /device:TPU:1, one launch (start us, length us, event | category | flops | bytes accessed | tf_op | source)
XLA Modules:
  0.0 751.1 jit_solution(14820244406813289233)
XLA Ops:
  7.2 0.0 copy-start
  7.2 0.0 all-gather.3.cloned.1.call-start
  7.2 0.7 all-gather.3.cloned.1.call-update
  7.9 1.8 reshape_squeeze.3
  9.7 11.6 %all-to-all-start = ((bf16[64,2,1280]{2,1,0:T(2,128)(2,1)}), bf16[64,2,1280]{2,1,0:T(2,128)(2,1)S(1)}, u32[]{:S(2)}, u32[]{:S(2)}) async-start(bf16[64,2,1280]{2,1,0:T(2,128)(2,1)} %reshape_squeeze.3), calls=%async_computation | async-start | bytes 655360 | tf_op jit(solution)/shard_map/all_to_all | solution.py:40
  21.4 89.6 %all-gather.3.cloned.1.call-done = bf16[64,20,3840]{2,1,0:T(8,128)(2,1)} async-done(((bf16[1,20,3840]{2,1,0:T(8,128)(2,1)}), bf16[64,20,3840]{2,1,0:T(8,128)(2,1)}) %all-gather.3.cloned.1.call-update) | async-done | bytes 9830416 | tf_op jit(solution)/shard_map/all_gather | solution.py:99
  110.9 13.7 %reshape.125 = bf16[1280,3840]{1,0:T(8,128)(2,1)} reshape(bf16[64,20,3840]{2,1,0:T(8,128)(2,1)} %all-gather.3.cloned.1.call-done) | data formatting | bytes 19660800
  124.6 0.0 copy-done
  124.6 7.1 convolution_convert_fusion.1
  131.7 0.1 reshape.83
  131.8 0.0 all-to-all-done
  131.8 19.7 %all_to_all.25 = bf16[64,2,1280]{2,1,0:T(2,128)(2,1)S(1)} all-to-all(bf16[64,2,1280]{2,1,0:T(2,128)(2,1)S(1)} %reshape.83), channel_id=1, replica_groups=mesh['dp'=8,'seq'=64] {'seq'}, dimensions={0} | all-to-all | bytes 655360 | tf_op jit(solution)/shard_map/all_to_all | solution.py:40
  151.5 5.0 stack.58
  156.6 5.5 all-to-all-start.2
  162.1 2.5 sort.17
  164.6 0.6 pad_clamp_fusion
  165.2 0.0 copy-done.4
  165.2 0.1 slice_reduce_fusion.25
  165.4 0.0 copy-start.16
  165.4 0.3 slice_reduce_fusion.26
  165.7 0.0 copy-start.5
  165.7 0.0 copy-start.6
  165.7 0.6 compare_and_fusion
  166.3 0.1 reshape.77
  166.4 0.9 gather_fusion
  167.3 0.1 reshape.84
  167.5 0.9 gather_fusion.2
  168.4 0.8 multiply_reduce_fusion
  169.2 2.5 collective-permute-start.1
  171.7 3.0 collective-permute-start
  174.8 0.7 slice_bitcast_fusion.1
  175.5 2.3 collective-permute-start.2
  177.8 2.2 collective-permute-start.3
  180.1 27.1 %collective-permute-done.1 = bf16[1,8,8,1280]{3,2,1,0:T(8,128)(2,1)S(1)} collective-permute-done((bf16[1,8,8,1280]{3,2,1,0:T(8,128)(2,1)S(1)}, bf16[1,8,8,1280]{3,2,1,0:T(8,128)(2,1)S(1)}, u32[]{:S(2)}, u32[]{:S(2)}) %collective-permute-start.1) | collective-permute-done | bytes 163872 | tf_op jit(solution)/shard_map/ppermute | solution.py:18
  207.1 0.0 collective-permute-done
  207.1 0.6 select_maximum_fusion.2
  207.8 2.4 fusion.83
  210.3 1.0 gather_fusion.1
  211.3 0.0 collective-permute-done.2
  211.3 0.0 collective-permute-done.3
  211.3 1.5 select_maximum_fusion
  212.8 3.4 add_convert_fusion
  216.2 1.7 gather_fusion.3
  217.9 1.8 broadcast_select_fusion
  219.7 0.8 reshape.80
  220.6 199.3 %all-to-all-done.2 = bf16[64,20,3840]{2,1,0:T(8,128)(2,1)} async-done(((bf16[64,20,3840]{2,1,0:T(8,128)(2,1)}), bf16[64,20,3840]{2,1,0:T(8,128)(2,1)}, u32[]{:S(2)}, u32[]{:S(2)}) %all-to-all-start.2) | async-done | bytes 9830432 | tf_op jit(solution)/shard_map/all_to_all | solution.py:115
  419.9 24.8 %all-to-all-start.1 = ((bf16[64,2,1280]{2,1,0:T(2,128)(2,1)}), bf16[64,2,1280]{2,1,0:T(2,128)(2,1)S(1)}, u32[]{:S(2)}, u32[]{:S(2)}) async-start(bf16[64,2,1280]{2,1,0:T(2,128)(2,1)} %reshape.80), calls=%async_computation.1 | async-start | bytes 655360 | tf_op jit(solution)/shard_map/all_to_all | solution.py:51
  444.7 0.0 copy-start.2
  444.7 13.7 %reshape.82 = bf16[1280,3840]{1,0:T(8,128)(2,1)} reshape(bf16[64,20,3840]{2,1,0:T(8,128)(2,1)} %all-to-all-done.2) | data formatting | bytes 19660800 | tf_op jit(solution)/shard_map/reshape | solution.py:114
  458.5 0.8 reshape.87
  459.3 1.8 fusion.82
  461.1 0.0 all-to-all-done.1
  461.2 10.3 %all-to-all-start.4 = ((bf16[64,2,1280]{2,1,0:T(2,128)(2,1)}), bf16[64,2,1280]{2,1,0:T(2,128)(2,1)S(1)}, u32[]{:S(2)}, u32[]{:S(2)}) async-start(bf16[64,2,1280]{2,1,0:T(2,128)(2,1)} %reshape.87), calls=%async_computation.4 | async-start | bytes 655360 | tf_op jit(solution)/shard_map/all_to_all | solution.py:51
  471.5 0.0 all-reduce.4.cloned.1.call-start
  471.5 0.6 fusion.78
  472.5 2.7 stack.86
  475.2 0.0 all-reduce.4.cloned.1.call-update
  475.2 0.1 reshape.81
  475.3 0.0 copy-start.1
  475.3 6.3 fusion
  481.6 4.0 all-to-all-done.4
  485.7 0.8 broadcast_in_dim_reshape.3
  486.5 256.1 %all-reduce.4.cloned.1.call-done = f32[27,1280]{1,0:T(8,128)} async-done(((f32[27,1280]{1,0:T(8,128)}), f32[27,1280]{1,0:T(8,128)}) %all-reduce.4.cloned.1.call-update) | async-done | bytes 138256 | tf_op jit(solution)/shard_map/psum | solution.py:120
  742.6 1.6 copy.9
  (65 shorter events, 0.3 us)
Async XLA Ops:
  7.2 117.5 %copy-start = (bf16[1,128,3840]{2,1,0:T(8,128)(2,1)S(1)}, bf16[1,128,3840]{2,1,0:T(8,128)(2,1)}, u32[]{:S(2)}) copy-start(bf16[1,128,3840]{2,1,0:T(8,128)(2,1)} %param.11) | copy-start | bytes 2949124
  7.2 103.8 %all-gather.3.cloned.1.call-start = ((), (), s32[]{:S(2)}) async-start(), calls=%async_computation.6 | async-start | bytes 11980800 | tf_op jit(solution)/shard_map/all_gather | solution.py:99
  9.7 122.1 %all-to-all-start = ((bf16[64,2,1280]{2,1,0:T(2,128)(2,1)}), bf16[64,2,1280]{2,1,0:T(2,128)(2,1)S(1)}, u32[]{:S(2)}, u32[]{:S(2)}) async-start(bf16[64,2,1280]{2,1,0:T(2,128)(2,1)} %reshape_squeeze.3), calls=%async_computation | async-start | bytes 655360 | tf_op jit(solution)/shard_map/all_to_all | solution.py:40
  124.6 26.9 %copy-start.3 = (bf16[20,3840]{1,0:T(8,128)(2,1)S(1)}, bf16[20,3840]{1,0:T(8,128)(2,1)}, u32[]{:S(2)}) copy-start(bf16[20,3840]{1,0:T(8,128)(2,1)} %param.10) | copy-start | bytes 460804
  156.5 5.5 copy-start.19
  156.5 8.7 %copy-start.4 = (f32[27,1280]{1,0:T(8,128)S(1)}, f32[27,1280]{1,0:T(8,128)}, u32[]{:S(2)}) copy-start(f32[27,1280]{1,0:T(8,128)} %param.9) | copy-start | bytes 414724
  156.6 263.3 %all-to-all-start.2 = ((bf16[64,20,3840]{2,1,0:T(8,128)(2,1)}), bf16[64,20,3840]{2,1,0:T(8,128)(2,1)}, u32[]{:S(2)}, u32[]{:S(2)}) async-start(bf16[64,20,3840]{2,1,0:T(8,128)(2,1)} %stack.58), calls=%async_computation.2 | async-start | bytes 23592960 | tf_op jit(solution)/shard_map/all_to_all | solution.py:115
  165.3 42.4 %copy-start.10 = (f32[1280]{0:T(1024)}, f32[1280]{0:T(1024)S(1)}, u32[]{:S(2)}) copy-start(f32[1280]{0:T(1024)S(1)} %get-tuple-element.57) | copy-start | bytes 15364
  165.3 42.4 %copy-start.11 = (f32[1280]{0:T(1024)}, f32[1280]{0:T(1024)S(1)}, u32[]{:S(2)}) copy-start(f32[1280]{0:T(1024)S(1)} %get-tuple-element.58) | copy-start | bytes 15364
  165.3 42.4 %copy-start.12 = (f32[1280]{0:T(1024)}, f32[1280]{0:T(1024)S(1)}, u32[]{:S(2)}) copy-start(f32[1280]{0:T(1024)S(1)} %get-tuple-element.59) | copy-start | bytes 15364
  165.3 42.4 %copy-start.13 = (f32[1280]{0:T(1024)}, f32[1280]{0:T(1024)S(1)}, u32[]{:S(2)}) copy-start(f32[1280]{0:T(1024)S(1)} %get-tuple-element.60) | copy-start | bytes 15364
  165.4 42.4 %copy-start.14 = (f32[1280]{0:T(1024)}, f32[1280]{0:T(1024)S(1)}, u32[]{:S(2)}) copy-start(f32[1280]{0:T(1024)S(1)} %get-tuple-element.61) | copy-start | bytes 15364
  165.4 42.4 %copy-start.15 = (f32[1280]{0:T(1024)}, f32[1280]{0:T(1024)S(1)}, u32[]{:S(2)}) copy-start(f32[1280]{0:T(1024)S(1)} %get-tuple-element.62) | copy-start | bytes 15364
  165.4 42.4 %copy-start.16 = (f32[1280]{0:T(1024)}, f32[1280]{0:T(1024)S(1)}, u32[]{:S(2)}) copy-start(f32[1280]{0:T(1024)S(1)} %get-tuple-element.63) | copy-start | bytes 15364
  165.4 42.4 %copy-start.17 = (f32[1280]{0:T(1024)}, f32[1280]{0:T(1024)S(1)}, u32[]{:S(2)}) copy-start(f32[1280]{0:T(1024)S(1)} %get-tuple-element.64) | copy-start | bytes 15364
  165.7 42.1 %copy-start.5 = (f32[1280]{0:T(1024)}, f32[1280]{0:T(1024)S(1)}, u32[]{:S(2)}) copy-start(f32[1280]{0:T(1024)S(1)} %get-tuple-element.52) | copy-start | bytes 15364
  165.7 42.1 %copy-start.6 = (f32[1280]{0:T(1024)}, f32[1280]{0:T(1024)S(1)}, u32[]{:S(2)}) copy-start(f32[1280]{0:T(1024)S(1)} %get-tuple-element.53) | copy-start | bytes 15364
  165.7 42.1 %copy-start.7 = (f32[1280]{0:T(1024)}, f32[1280]{0:T(1024)S(1)}, u32[]{:S(2)}) copy-start(f32[1280]{0:T(1024)S(1)} %get-tuple-element.54) | copy-start | bytes 15364
  165.7 42.1 %copy-start.8 = (f32[1280]{0:T(1024)}, f32[1280]{0:T(1024)S(1)}, u32[]{:S(2)}) copy-start(f32[1280]{0:T(1024)S(1)} %get-tuple-element.55) | copy-start | bytes 15364
  165.7 42.1 %copy-start.9 = (f32[1280]{0:T(1024)}, f32[1280]{0:T(1024)S(1)}, u32[]{:S(2)}) copy-start(f32[1280]{0:T(1024)S(1)} %get-tuple-element.56) | copy-start | bytes 15364
  169.2 37.9 %collective-permute-start.1 = (bf16[1,8,8,1280]{3,2,1,0:T(8,128)(2,1)S(1)}, bf16[1,8,8,1280]{3,2,1,0:T(8,128)(2,1)S(1)}, u32[]{:S(2)}, u32[]{:S(2)}) collective-permute-start(bf16[1,8,8,1280]{3,2,1,0:T(8,128)(2,1)S(1)} %get-tuple-element.70), channel_id=1, source_target_pairs={{1,0},{2,1},{3,2},{4,3},{5,4},{6,5},{7,6},{8,7},{9,8},{10,9},{11,1... | collective-permute-start | bytes 491528 | tf_op jit(solution)/shard_map/ppermute | solution.py:18
  171.7 35.4 %collective-permute-start = (bf16[1,8,8,1280]{3,2,1,0:T(8,128)(2,1)S(1)}, bf16[1,8,8,1280]{3,2,1,0:T(8,128)(2,1)S(1)}, u32[]{:S(2)}, u32[]{:S(2)}) collective-permute-start(bf16[1,8,8,1280]{3,2,1,0:T(8,128)(2,1)S(1)} %get-tuple-element.71), channel_id=1, source_target_pairs={{0,1},{1,2},{2,3},{3,4},{4,5},{5,6},{6,7},{7,8},{8,9},{9,10},{10,1... | collective-permute-start | bytes 491528 | tf_op jit(solution)/shard_map/ppermute | solution.py:17
  175.5 35.8 %collective-permute-start.2 = (bf16[1,8,8,1280]{3,2,1,0:T(8,128)(2,1)}, bf16[1,8,8,1280]{3,2,1,0:T(8,128)(2,1)S(1)}, u32[]{:S(2)}, u32[]{:S(2)}) collective-permute-start(bf16[1,8,8,1280]{3,2,1,0:T(8,128)(2,1)} %get-tuple-element.68), channel_id=1, source_target_pairs={{0,1},{1,2},{2,3},{3,4},{4,5},{5,6},{6,7},{7,8},{8,9},{9,10},{10,1... | collective-permute-start | bytes 491528 | tf_op jit(solution)/shard_map/ppermute | solution.py:17
  177.8 33.5 %collective-permute-start.3 = (bf16[1,8,8,1280]{3,2,1,0:T(8,128)(2,1)}, bf16[1,8,8,1280]{3,2,1,0:T(8,128)(2,1)}, u32[]{:S(2)}, u32[]{:S(2)}) collective-permute-start(bf16[1,8,8,1280]{3,2,1,0:T(8,128)(2,1)} %get-tuple-element.69), channel_id=1, source_target_pairs={{1,0},{2,1},{3,2},{4,3},{5,4},{6,5},{7,6},{8,7},{9,8},{10,9},{11,1... | collective-permute-start | bytes 491528 | tf_op jit(solution)/shard_map/ppermute | solution.py:18
  419.9 41.3 %all-to-all-start.1 = ((bf16[64,2,1280]{2,1,0:T(2,128)(2,1)}), bf16[64,2,1280]{2,1,0:T(2,128)(2,1)S(1)}, u32[]{:S(2)}, u32[]{:S(2)}) async-start(bf16[64,2,1280]{2,1,0:T(2,128)(2,1)} %reshape.80), calls=%async_computation.1 | async-start | bytes 655360 | tf_op jit(solution)/shard_map/all_to_all | solution.py:51
  444.7 13.7 %copy-start.18 = (f32[1280]{0:T(1024)S(1)}, f32[1280]{0:T(1024)}, u32[]{:S(2)}) copy-start(f32[1280]{0:T(1024)} %get-tuple-element.65) | copy-start | bytes 15364
  444.7 13.7 %copy-start.2 = (bf16[128,1280]{1,0:T(8,128)(2,1)S(1)}, bf16[128,1280]{1,0:T(8,128)(2,1)}, u32[]{:S(2)}) copy-start(bf16[128,1280]{1,0:T(8,128)(2,1)} %get-tuple-element.72) | copy-start | bytes 983044
  461.2 24.5 %all-to-all-start.4 = ((bf16[64,2,1280]{2,1,0:T(2,128)(2,1)}), bf16[64,2,1280]{2,1,0:T(2,128)(2,1)S(1)}, u32[]{:S(2)}, u32[]{:S(2)}) async-start(bf16[64,2,1280]{2,1,0:T(2,128)(2,1)} %reshape.87), calls=%async_computation.4 | async-start | bytes 655360 | tf_op jit(solution)/shard_map/all_to_all | solution.py:51
  471.5 271.1 %all-reduce.4.cloned.1.call-start = ((), (), s32[]{:S(2)}) async-start(), calls=%async_computation.5 | async-start | bytes 327680 | tf_op jit(solution)/shard_map/psum | solution.py:120
  475.3 268.9 %copy-start.1 = (bf16[1,128,3840]{2,1,0:T(8,128)(2,1)S(1)}, bf16[1,128,3840]{2,1,0:T(8,128)(2,1)}, u32[]{:S(2)}) copy-start(bf16[1,128,3840]{2,1,0:T(8,128)(2,1)} %param.11) | copy-start | bytes 2949124
Sparse Core Ops, SparseCore 0:
  11.3 99.6 all-gather.2
  477.9 264.6 all-reduce.3
